TPU v7x, 512 devices: a whole 4x4x16 slice. The times are simulated.
512 devices in a mesh: wide: 64 (over z_lo, x, core), rows: 8 (over z_hi, y).
Axes of the slice: x: 4, y: 4, z: 16 (z_hi: 2, z_lo: 8; z = z_hi * 8 + z_lo), core: 2. Of those that a mesh axis runs over, the one named last changes fastest.
Arguments:
- cotangent: float32 [2, 32768, 3072], P(None, 'wide', 'rows'), may hold values from -6 to 6
- amplitude: bfloat16 [256, 256, 3072], P('wide', None, 'rows'), may hold values from 0.099609375 to 2
- view_phase: bfloat16 [256, 256, 3072], P('wide', None, 'rows'), may hold values from -3.140625 to 3.140625
- layer_block: int32 [256, 256, 384], P('wide', None, 'rows'), may hold values from 0 to 8
- layer_phase: float32 [8, 256], P(None, 'wide'), may hold values from -3.140625 to 3.140625
Outputs:
- grad_amplitude: bfloat16 [256, 256, 3072], P('wide', None, 'rows')
- grad_phase: bfloat16 [256, 256, 3072], P('wide', None, 'rows')
- grad_layers: float32 [8, 256], P(None, 'wide')
Inputs may be any that keep to these rules, and one draw needn't show every extreme that they name: `layer_block`: value 8 marks a view occluded in that block of 8 rows.
All inputs are finite; a program needn't handle non-finite values.
Results may differ from a plain program's by a relative error of at most 0.0049.
Values may be sent and summed in bfloat16 or wider, within the bound.
A program may use at most 64 MiB of HBM per device.

v0:
```python
import math

import jax
import jax.numpy as jnp
from jax import lax
from jax.sharding import PartitionSpec as P

HOG = 256
LAYERS = 8
BLOCK = 8


def from_behind(value, axis, by):
    devices = lax.axis_size(axis)
    pairs = [(i, i + by) for i in range(devices) if 0 <= i + by < devices]
    return lax.ppermute(value, axis, pairs)


def fourier_table():
    index = jnp.arange(HOG, dtype=jnp.int32)
    product = index[:, None] * index[None, :] % HOG
    angles = 2.0 * math.pi / HOG * product.astype(jnp.float32)
    samples = index.astype(jnp.float32)
    window = jnp.sin(math.pi * (samples + 0.5) / HOG) ** 2 / math.sqrt(HOG)
    cosine = jnp.cos(angles) * window[None, :]
    sine_part = jnp.sin(angles) * window[None, :]
    return jnp.stack([jnp.stack([cosine, sine_part], 1), jnp.stack([-sine_part, cosine], 1)], 0)


def half_product(table_half, frames):
    return jnp.einsum("pkqn,qhnr->pkhr", table_half, frames, precision=lax.Precision.HIGHEST)


def spectra_of(table, leading, trailing):
    half_hogel = HOG // 2
    return half_product(table[..., :half_hogel], leading) + half_product(
        table[..., half_hogel:], trailing
    )


def view_gradients(real_part, imag_part, amplitude, view_phase, layer_here, phase_table):
    layers_rows = jnp.repeat(layer_here, BLOCK, axis=2)
    visible = (layers_rows < LAYERS).astype(jnp.float32)
    lookup = jnp.zeros(layers_rows.shape, jnp.float32)
    for level in range(LAYERS):
        lookup = lookup + jnp.where(layers_rows == level, phase_table[level][:, None, None], 0.0)
    angles = view_phase.astype(jnp.float32) + lookup
    cosine = jnp.cos(angles)
    sine_part = jnp.sin(angles)
    real_f = real_part.astype(jnp.float32)
    imag_f = imag_part.astype(jnp.float32)
    grad_amp = visible * (real_f * cosine + imag_f * sine_part)
    phase_term = visible * amplitude.astype(jnp.float32) * (imag_f * cosine - real_f * sine_part)
    table_part = jnp.stack(
        [
            jnp.sum(jnp.where(layers_rows == level, phase_term, 0.0), (1, 2))
            for level in range(LAYERS)
        ],
        0,
    )
    return (grad_amp.astype(jnp.bfloat16), phase_term.astype(jnp.bfloat16), table_part)


def shards(cotangent, amplitude, view_phase, layer_block, layer_phase):
    half_hogel = HOG // 2
    table = fourier_table()
    columns = cotangent.shape[1]
    rows_here = cotangent.shape[2]
    count = columns // half_hogel
    right_edge = from_behind(cotangent[:, :half_hogel, :], "wide", -1)
    extended = jnp.concatenate([cotangent, right_edge], 1)
    leading = extended[:, : count * half_hogel, :].reshape(2, count, half_hogel, rows_here)
    trailing = extended[:, half_hogel:, :].reshape(2, count, half_hogel, rows_here)
    spectra = spectra_of(table, leading, trailing)
    spectra = spectra.astype(jnp.bfloat16)
    relayed = lax.all_to_all(spectra, "wide", split_axis=1, concat_axis=2, tiled=True)
    grad_amp, grad_ph, table_part = view_gradients(
        relayed[0], relayed[1], amplitude, view_phase, layer_block, layer_phase
    )
    total = lax.psum(table_part, "rows")
    norm_factor = 1.0 / math.sqrt(amplitude.shape[2] * lax.axis_size("rows") * amplitude.shape[1])
    return (grad_amp, grad_ph, total * norm_factor)


def solution(mesh):
    in_specs = (
        P(None, "wide", "rows"),
        P("wide", None, "rows"),
        P("wide", None, "rows"),
        P("wide", None, "rows"),
        P(None, "wide"),
    )
    out_specs = (P("wide", None, "rows"), P("wide", None, "rows"), P(None, "wide"))
    return jax.shard_map(shards, mesh=mesh, in_specs=in_specs, out_specs=out_specs, check_vma=False)
```

profile of v0, /device:TPU:6, one launch (start us, length us, event | category | flops | bytes accessed | tf_op | source)
XLA Modules:
  0.0 167.5 jit_solution(1212989035608598141)
XLA Ops:
  0.6 0.0 copy-start
  0.6 1.1 slice.46
  1.8 2.2 %collective-permute-start = (f32[2,128,384]{2,1,0:T(8,128)S(1)}, f32[2,128,384]{2,1,0:T(8,128)S(1)}, u32[]{:S(2)}, u32[]{:S(2)}) collective-permute-start(f32[2,128,384]{2,1,0:T(8,128)S(1)} %slice.46), channel_id=1, source_target_pairs={{8,0},{16,8},{24,16},{32,24},{40,32},{48,40},{56,48},{64,56},{72,6... | collective-permute-start | bytes 1179656 | tf_op jit(solution)/shard_map/ppermute | solution.py:16
  4.0 1.1 fusion.36
  5.1 0.1 maximum_bitcast_fusion.1
  5.2 0.0 copy-done
  5.2 2.8 %fusion.20 = f32[2,256,4,384,1]{3,1,4,2,0:T(8,128)S(1)} fusion(f32[2,4,128,384]{3,2,1,0:T(8,128)S(1)} %bitcast.134, f32[1,256,2,256]{3,1,2,0:T(8,128)S(1)} %get-tuple-element.38, f32[1,256,2,256]{3,1,2,0:T(8,128)S(1)} %get-tuple-element.37), kind=kOutput, calls=%fused_computation.40 | convolution fusion | flops 2416050176 | bytes 5767168 | tf_op jit(solution)/shard_map/pkqn,qhnr->pkhr/dot_general | solution.py:31
  8.0 1.2 collective-permute-done
  9.2 0.1 pad_maximum_fusion
  9.4 3.0 %fusion = bf16[2,256,4,384]{3,1,2,0:T(8,128)(2,1)S(1)} fusion(f32[2,256,4,384,1]{3,1,4,2,0:T(8,128)S(1)} %fusion.20, f32[2,4,128,384]{3,2,1,0:T(8,128)S(1)} %bitcast.135, f32[1,256,2,256]{3,1,2,0:T(8,128)S(1)} %get-tuple-element.37, f32[1,256,2,256]{3,1,2,0:T(8,128)S(1)} %get-tuple-element.38), kind=kOutput, calls=%fused_computation.1 | convolution fusion | flops 2417623040 | bytes 7340032 | tf_op jit(solution)/shard_map/pkqn,qhnr->pkhr/dot_general | solution.py:31
  12.3 2.4 %copy.44 = bf16[2,256,4,384]{3,2,0,1:T(4,128)(2,1)} copy(bf16[2,256,4,384]{3,1,2,0:T(8,128)(2,1)S(1)} %fusion) | data formatting | bytes 3145728 | tf_op jit(solution)/shard_map/convert_element_type | solution.py:75
  14.7 17.7 %all-to-all-start = ((bf16[2,256,4,384]{3,2,0,1:T(4,128)(2,1)}), bf16[2,256,4,384]{3,2,0,1:T(4,128)(2,1)S(1)}, u32[]{:S(2)}, u32[]{:S(2)}) async-start(bf16[2,256,4,384]{3,2,0,1:T(4,128)(2,1)} %copy.44), calls=%async_computation | async-start | bytes 3145728 | tf_op jit(solution)/shard_map/all_to_all | solution.py:76
  32.4 0.0 copy-start.4
  32.4 0.3 copy.46
  32.7 0.0 copy-start.3
  32.7 2.3 %copy.49 = bf16[4,256,384]{1,2,0:T(8,128)(2,1)} copy(bf16[4,256,384]{2,1,0:T(8,128)(2,1)} %param.6) | data formatting | bytes 1572864 | tf_op args[1]
  35.1 0.0 copy-done.4
  35.1 0.3 slice_reduce_fusion.7
  35.4 0.9 broadcast_compare_fusion.8
  36.2 8.0 %fusion.40 = (f32[4,256,384]{1,2,0:T(8,128)}, f32[4,256,384]{1,2,0:T(8,128)}) fusion(f32[4]{0:T(128)S(1)} %get-tuple-element.29, pred[4,256,48]{1,2,0:T(8,128)(4,1)S(1)} %get-tuple-element.46, f32[4]{0:T(128)S(1)} %get-tuple-element.30, pred[4,256,48]{1,2,0:T(8,128)(4,1)S(1)} %get-tuple-element.47, f32[4]{0:T(128)S(1)} %get-tuple-element.24, ...), kind=kLoop, calls=%fused_computation.89 | loop fusion | flops 6684672 | bytes 4325504 | tf_op jit(solution)/shard_map/cos | solution.py:48
  44.2 62.0 %all-to-all-done = bf16[2,256,4,384]{3,2,0,1:T(4,128)(2,1)S(1)} async-done(((bf16[2,256,4,384]{3,2,0,1:T(4,128)(2,1)}), bf16[2,256,4,384]{3,2,0,1:T(4,128)(2,1)S(1)}, u32[]{:S(2)}, u32[]{:S(2)}) %all-to-all-start) | async-done | bytes 1572896 | tf_op jit(solution)/shard_map/all_to_all | solution.py:76
  106.2 0.6 copy.68
  106.8 0.5 fusion.42
  107.3 0.6 bitcast_convert_fusion
  107.9 1.7 copy.47
  109.6 1.6 copy.48
  111.2 10.1 %fusion.18 = (f32[4]{0:T(128)S(1)}, f32[4]{0:T(128)S(1)}, f32[4]{0:T(128)S(1)}, f32[4]{0:T(128)S(1)}, f32[4]{0:T(128)}, /*index=5*/f32[4]{0:T(128)}, f32[4]{0:T(...) fusion(pred[4,256,48]{1,2,0:T(8,128)(4,1)S(1)} %get-tuple-element.46, ...), kind=kLoop, calls=%fused_computation.37 | loop fusion | flops 11010016 | bytes 9093248 | tf_op jit(solution)/shard_map/reduce_sum | solution.py:56
  121.4 1.2 copy.52
  122.5 1.2 copy.53
  123.7 0.0 copy-done.8
  123.7 43.1 %psum.7 = f32[8,4]{1,0:T(8,128)S(1)} all-reduce(f32[8,4]{1,0:T(8,128)S(1)} %stack.59), channel_id=1, replica_groups=mesh['wide'=64,'rows'=8] {'rows'}, use_global_device_ids=true, to_apply=%region_8.9 | all-reduce | flops 32 | bytes 256 | tf_op jit(solution)/shard_map/psum | solution.py:80
  166.8 0.7 copy.54
  (15 shorter events, 0.1 us)
Async XLA Ops:
  0.6 4.5 %copy-start = (f32[2,512,384]{2,1,0:T(8,128)S(1)}, f32[2,512,384]{2,1,0:T(8,128)}, u32[]{:S(2)}) copy-start(f32[2,512,384]{2,1,0:T(8,128)} %param.5) | copy-start | bytes 4718596
  1.8 7.5 %collective-permute-start = (f32[2,128,384]{2,1,0:T(8,128)S(1)}, f32[2,128,384]{2,1,0:T(8,128)S(1)}, u32[]{:S(2)}, u32[]{:S(2)}) collective-permute-start(f32[2,128,384]{2,1,0:T(8,128)S(1)} %slice.46), channel_id=1, source_target_pairs={{8,0},{16,8},{24,16},{32,24},{40,32},{48,40},{56,48},{64,56},{72,6... | collective-permute-start | bytes 1179656 | tf_op jit(solution)/shard_map/ppermute | solution.py:16
  14.7 17.7 %copy-start.2 = (bf16[4,256,384]{2,1,0:T(8,128)(2,1)S(1)}, bf16[4,256,384]{2,1,0:T(8,128)(2,1)}, u32[]{:S(2)}) copy-start(bf16[4,256,384]{2,1,0:T(8,128)(2,1)} %param.7) | copy-start | bytes 2359300
  14.7 91.5 %all-to-all-start = ((bf16[2,256,4,384]{3,2,0,1:T(4,128)(2,1)}), bf16[2,256,4,384]{3,2,0,1:T(4,128)(2,1)S(1)}, u32[]{:S(2)}, u32[]{:S(2)}) async-start(bf16[2,256,4,384]{3,2,0,1:T(4,128)(2,1)} %copy.44), calls=%async_computation | async-start | bytes 3145728 | tf_op jit(solution)/shard_map/all_to_all | solution.py:76
  32.4 2.6 %copy-start.4 = (f32[8,4]{0,1:T(4,128)S(1)}, f32[8,4]{0,1:T(4,128)}, u32[]{:S(2)}) copy-start(f32[8,4]{0,1:T(4,128)} %param.9) | copy-start | bytes 388
  32.7 2.6 %copy-start.3 = (s32[4,256,48]{1,2,0:T(8,128)S(1)}, s32[4,256,48]{1,2,0:T(8,128)}, u32[]{:S(2)}) copy-start(s32[4,256,48]{1,2,0:T(8,128)} %param.8) | copy-start | bytes 589828
  109.6 1.6 copy-start.1
  121.4 2.3 %copy-start.5 = (f32[4]{0:T(128)S(1)}, f32[4]{0:T(128)}, u32[]{:S(2)}) copy-start(f32[4]{0:T(128)} %get-tuple-element.19) | copy-start | bytes 52
  121.4 2.3 %copy-start.6 = (f32[4]{0:T(128)S(1)}, f32[4]{0:T(128)}, u32[]{:S(2)}) copy-start(f32[4]{0:T(128)} %get-tuple-element.20) | copy-start | bytes 52
  121.4 2.3 %copy-start.7 = (f32[4]{0:T(128)S(1)}, f32[4]{0:T(128)}, u32[]{:S(2)}) copy-start(f32[4]{0:T(128)} %get-tuple-element.21) | copy-start | bytes 52
  121.4 2.3 %copy-start.8 = (f32[4]{0:T(128)S(1)}, f32[4]{0:T(128)}, u32[]{:S(2)}) copy-start(f32[4]{0:T(128)} %get-tuple-element.22) | copy-start | bytes 52
where the time goes:
time: 168 us; the launch traced here: 167 us
  waiting for transfers between devices  63.2 us (38%)
  blocking collectives  43.1 us (26%)
  other arithmetic  20.9 us (12%)
  starting transfers between devices  19.9 us (12%)
  local copies, waits for them, and re-layouts  13.9 us (8%)
  matrix products  5.78 us (3%)
    all_to_all x1, waiting for transfers between devices, shards(): lax.all_to_all(spectra, 'wide', split_axis=1, concat_axis=2, tiled=True)  62 us
    psum x1, blocking collectives, shards(): total = lax.psum(table_part, 'rows')  43.1 us
    all_to_all x1, starting transfers between devices, shards(): lax.all_to_all(spectra, 'wide', split_axis=1, concat_axis=2, tiled=True)  17.7 us
    reduce_sum x1, other arithmetic, view_gradients(): jnp.sum(jnp.where(layers_rows == level, phase_term, 0.0), (1, 2))  10.1 us
    cos x1, other arithmetic, view_gradients(): cosine = jnp.cos(angles)  7.96 us
    dot_general x2, matrix products, half_product(): jnp.einsum('pkqn,qhnr->pkhr', table_half, frames, precision=lax.Precision...  5.78 us
    unnamed x23, local copies, waits for them, and re-layouts  5.61 us
  transfers between devices with their start and end apart: 2, of which 2 were waited for; matrix products, arithmetic and copies ran while one was open for 9% of the time, Pallas kernels for 0%

commit v1 on v0

v1 whole, which is shorter than its diff:
```python
import functools
import math

import jax
import jax.numpy as jnp
import numpy as np
from jax import lax
from jax.experimental import pallas as pl
from jax.experimental.pallas import tpu as pltpu
from jax.sharding import PartitionSpec as P

MESH = pl.DeviceIdType.MESH
HOG = 256
HALF = HOG // 2
LAYERS = 8
BLOCK = 8
WIDE = 64
ROWS = 8
VIEWS = 4
HOGELS = 4
NR = 384
NB = NR // BLOCK
NH = 256
GROUP = 4
GROUPS = WIDE // GROUP
COS = (0.999999989, -0.499999891, 0.0416664892, -0.00138878035, 2.47698825e-05, -2.70790202e-07, 1.72450525e-09)
SIN = (0.999999999, -0.166666659, 0.00833332129, -0.000198405341, 2.75358492e-06, -2.47288044e-08, 1.36130722e-10)


def fourier_table():
    index = np.arange(HOG)
    angles = 2.0 * math.pi / HOG * (index[:, None] * index[None, :] % HOG)
    window = np.sin(math.pi * (index + 0.5) / HOG) ** 2 / math.sqrt(HOG)
    cosine = np.cos(angles) * window[None, :]
    sine = np.sin(angles) * window[None, :]
    table = np.stack([np.stack([cosine, sine], 1), np.stack([-sine, cosine], 1)], 0)
    table = table.reshape(2, WIDE, VIEWS, 2 * HOG).swapaxes(0, 1).reshape(2 * HOG, 2 * HOG)
    return table.astype(np.float32)


def places(shape):
    return (lax.broadcasted_iota(jnp.int32, shape, axis) for axis in range(2))


def ones_where(chosen):
    return jnp.where(chosen, 1.0, 0.0).astype(jnp.bfloat16)


def gather_order():
    goes, came = places((128, 128))
    part, view, source, half, hogel = goes >> 6, (goes >> 4) & 3, (goes >> 2) & 3, (goes >> 1) & 1, goes & 1
    return ones_where(came == half * 64 + source * 16 + hogel * 8 + part * 4 + view)


def polynomial(coefficients, square):
    total = jnp.full_like(square, coefficients[-1])
    for coefficient in coefficients[-2::-1]:
        total = total * square + coefficient
    return total


def cos_sin(angle):
    square = angle * angle
    return polynomial(COS, square), angle * polynomial(SIN, square)


def halves(value):
    high = value.astype(jnp.bfloat16)
    return high, (value - high.astype(jnp.float32)).astype(jnp.bfloat16)


def dot(a, b):
    return jnp.dot(a, b, preferred_element_type=jnp.float32)


def kernel(
    cot_hbm, amp_hbm, phase_hbm, layer_hbm, table_ref, fourier_hbm,
    grad_amp_hbm, grad_phase_hbm, grad_layers_ref,
    cot, amp, phase, layer_in, fourier, layer, thigh, tlow, spread, gather, order,
    xhigh, xlow, stage, recv, cosines, sines, grad_amp, grad_phase, sums, partial,
    load_sem, send_sem, recv_sem, own_sem, halo_send, halo_recv, out_sem, row_send, row_recv,
):
    me = lax.axis_index("wide")
    row = lax.axis_index("rows")

    barrier = pltpu.get_barrier_semaphore()

    def greet_wide(n, carry):
        other = lax.rem(me + n, WIDE)
        pl.semaphore_signal(barrier, inc=1, device_id={"wide": other}, device_id_type=MESH)
        return carry

    lax.fori_loop(1, WIDE, greet_wide, 0)
    for n in range(1, ROWS):
        pl.semaphore_signal(barrier, inc=1, device_id={"rows": lax.rem(row + n, ROWS)}, device_id_type=MESH)

    loads = [
        pltpu.make_async_copy(source, target, load_sem.at[i])
        for i, (source, target) in enumerate(
            (
                (cot_hbm, cot), (fourier_hbm, fourier), (amp_hbm, amp), (phase_hbm, phase), (layer_hbm, layer_in),
            )
        )
    ]
    for load in loads:
        load.start()
    loads[0].wait()
    high, low = halves(cot[...])
    xhigh[:, : HOGELS * HALF, :] = high
    xlow[...] = low
    loads[1].wait()
    thigh[...], tlow[...] = halves(fourier[...])

    def transform(hogel):
        total = None
        for q in range(2):
            columns = pl.ds(q * HOG, HOG)
            upper = xhigh[q, hogel * HALF : hogel * HALF + HOG, :]
            terms = [dot(thigh[:, columns], upper), dot(tlow[:, columns], upper)]
            if hogel < HOGELS - 1:
                terms.append(dot(thigh[:, columns], xlow[q, hogel * HALF : hogel * HALF + HOG, :]))
            else:
                terms.append(dot(thigh[:, q * HOG : q * HOG + HALF], xlow[q, hogel * HALF :, :]))
            for term in terms:
                total = term if total is None else total + term
        return total.reshape(WIDE, 8, NR)

    def send(half, n):
        other = lax.rem(me + n, WIDE)
        return pltpu.make_async_remote_copy(
            src_ref=stage.at[half, other], dst_ref=recv.at[half, me], send_sem=send_sem.at[half],
            recv_sem=recv_sem.at[half, me], device_id={"wide": other}, device_id_type=MESH,
        )

    def keep(half):
        return pltpu.make_async_copy(stage.at[half, me], recv.at[half, me], own_sem.at[half])

    def each_send(half, act):
        def step(n, carry):
            act(send(half, n))
            return carry

        lax.fori_loop(1, WIDE, step, 0)

    halo = pltpu.make_async_remote_copy(
        src_ref=xhigh.at[:, pl.ds(0, HALF)], dst_ref=xhigh.at[:, pl.ds(HOGELS * HALF, HALF)],
        send_sem=halo_send, recv_sem=halo_recv,
        device_id={"wide": lax.rem(me + WIDE - 1, WIDE)}, device_id_type=MESH,
    )

    stage[0] = jnp.concatenate([transform(0), transform(1)], 1).astype(jnp.bfloat16)
    pl.semaphore_wait(barrier, WIDE - 1 + ROWS - 1)

    @pl.when(me > 0)
    def _():
        halo.start()

    each_send(0, lambda copy: copy.start())
    keep(0).start()
    second = transform(2)

    @pl.when(me < WIDE - 1)
    def _():
        halo.wait_recv()

    @pl.when(me == WIDE - 1)
    def _():
        xhigh[:, pl.ds(HOGELS * HALF, HALF), :] = jnp.zeros((2, HALF, NR), jnp.bfloat16)

    stage[1] = jnp.concatenate([second, transform(3)], 1).astype(jnp.bfloat16)
    each_send(1, lambda copy: copy.start())
    keep(1).start()

    for load in loads[2:]:
        load.wait()
    sums[...] = jnp.zeros_like(sums)
    order[...] = gather_order()
    block, sample = places((NB, NR))
    spread[...] = ones_where(block == sample >> 3)
    sample, block = places((NR, NB))
    gather[...] = ones_where(block == sample >> 3)
    left, right = places((NB, NB))
    same = ones_where(left == right)

    def turned(value, by):
        return lax.dot_general(value, by, (((0,), (0,)), ((), ())), preferred_element_type=jnp.float32)

    for view in range(VIEWS):
        level = layer_in[view]
        layer[view] = turned(level.astype(jnp.float32).astype(jnp.bfloat16), same)
        added = jnp.zeros(level.shape, jnp.float32)
        for l in range(LAYERS):
            added = jnp.where(level == l, table_ref[view, l], added)
        cosine, sine = cos_sin(added)
        seen = level < LAYERS
        cosines[view] = sum(turned(part, spread[...]) for part in halves(jnp.where(seen, cosine, 0.0)))
        sines[view] = sum(turned(part, spread[...]) for part in halves(jnp.where(seen, sine, 0.0)))

    def angles(group, carry):
        here = pl.ds(pl.multiple_of(group * 16, 16), 16)
        own_cosine, own_sine = cos_sin(phase[:, here, :].astype(jnp.float32))
        wide_cosine, wide_sine = cosines[:, here, :], sines[:, here, :]
        cosines[:, here, :] = own_cosine * wide_cosine - own_sine * wide_sine
        sines[:, here, :] = own_sine * wide_cosine + own_cosine * wide_sine
        return carry

    lax.fori_loop(0, GROUPS, angles, 0)

    def finished(group):
        here = pl.ds(pl.multiple_of(group * 16, 16), 16)
        return [
            pltpu.make_async_copy(source.at[:, here], target.at[:, here], out_sem.at[i])
            for i, (source, target) in enumerate(((grad_amp, grad_amp_hbm), (grad_phase, grad_phase_hbm)))
        ]

    keep(0).wait()
    keep(1).wait()

    def gradients(n, carry):
        group = lax.rem(me // GROUP + GROUPS - n, GROUPS)
        here = pl.ds(pl.multiple_of(group * 16, 16), 16)
        for source in range(GROUP):
            index = group * GROUP + source

            @pl.when(index != me)
            def _():
                for half in range(2):
                    landed = recv.at[half, index]
                    pltpu.make_async_copy(landed, landed, recv_sem.at[half, index]).wait()

        came = recv[:, pl.ds(group * GROUP, GROUP), :, :].reshape(2 * GROUP * 16, NR)
        ordered = dot(order[...], came)
        real = ordered[:64].reshape(VIEWS, 16, NR)
        imag = ordered[64:].reshape(VIEWS, 16, NR)
        cosine = cosines[:, here, :]
        sine = sines[:, here, :]
        grad_amp[:, here, :] = (real * cosine + imag * sine).astype(jnp.bfloat16)
        term = amp[:, here, :].astype(jnp.float32) * (imag * cosine - real * sine)
        grad_phase[:, here, :] = term.astype(jnp.bfloat16)
        for copy in finished(group):
            copy.start()
        flat = term.reshape(VIEWS * 16, NR)
        blocks = sum(dot(part, gather[...]) for part in halves(flat)).reshape(VIEWS, 16, NB)
        level = layer[:, here, :]
        for l in range(LAYERS):
            chosen = jnp.where(level == float(l), blocks, 0.0)
            sums[l] += chosen[:, :8, :] + chosen[:, 8:, :]
        return carry

    lax.fori_loop(0, GROUPS, gradients, 0)

    view_of, level_of = places((8, 128))
    own = jnp.zeros((8, 128), jnp.float32)
    for l in range(LAYERS):
        lane = jnp.sum(jnp.sum(sums[l], axis=1), axis=1, keepdims=True)
        lane = jnp.concatenate([lane, jnp.zeros((8 - VIEWS, 1), jnp.float32)], 0)
        own = jnp.where(level_of == l, lane, own)
    partial[0] = own
    for n in range(1, ROWS):
        pltpu.make_async_remote_copy(
            src_ref=partial.at[0], dst_ref=partial.at[n], send_sem=row_send.at[n], recv_sem=row_recv.at[n],
            device_id={"rows": lax.rem(row + n, ROWS)}, device_id_type=MESH,
        ).start()

    for half in range(2):
        each_send(half, lambda copy: copy.wait_send())

    @pl.when(me > 0)
    def _():
        halo.wait_send()

    total = own
    for n in range(1, ROWS):
        pltpu.make_async_copy(partial.at[n], partial.at[n], row_recv.at[n]).wait()
    for n in range(1, ROWS):
        total = total + partial[n]
        pltpu.make_async_copy(partial.at[0], partial.at[0], row_send.at[n]).wait()
    grad_layers_ref[...] = (total * (1.0 / math.sqrt(NR * ROWS * NH)))[:VIEWS, :LAYERS]

    for copy in [
        pltpu.make_async_copy(grad_amp, grad_amp_hbm, out_sem.at[0]),
        pltpu.make_async_copy(grad_phase, grad_phase_hbm, out_sem.at[1]),
    ]:
        copy.wait()


def shards(cotangent, amplitude, view_phase, layer_block, layer_phase):
    anywhere = pl.BlockSpec(memory_space=pl.ANY)
    bf16, f32 = jnp.bfloat16, jnp.float32
    dma = pltpu.SemaphoreType.DMA
    grad_amp, grad_phase, grad_layers = pl.pallas_call(
        kernel,
        out_shape=(
            jax.ShapeDtypeStruct((VIEWS, NH, NR), bf16),
            jax.ShapeDtypeStruct((VIEWS, NH, NR), bf16),
            jax.ShapeDtypeStruct((VIEWS, LAYERS), f32),
        ),
        in_specs=[anywhere] * 4 + [pl.BlockSpec(memory_space=pltpu.SMEM), anywhere],
        out_specs=(anywhere, anywhere, pl.BlockSpec(memory_space=pltpu.VMEM)),
        scratch_shapes=[
            pltpu.VMEM((2, HOGELS * HALF, NR), f32),
            pltpu.VMEM((VIEWS, NH, NR), bf16),
            pltpu.VMEM((VIEWS, NH, NR), bf16),
            pltpu.VMEM((VIEWS, NB, NH), jnp.int32),
            pltpu.VMEM((2 * HOG, 2 * HOG), f32),
            pltpu.VMEM((VIEWS, NH, NB), f32),
            pltpu.VMEM((2 * HOG, 2 * HOG), bf16),
            pltpu.VMEM((2 * HOG, 2 * HOG), bf16),
            pltpu.VMEM((NB, NR), bf16),
            pltpu.VMEM((NR, NB), bf16),
            pltpu.VMEM((128, 128), bf16),
            pltpu.VMEM((2, (HOGELS + 1) * HALF, NR), bf16),
            pltpu.VMEM((2, HOGELS * HALF, NR), bf16),
            pltpu.VMEM((2, WIDE, 16, NR), bf16),
            pltpu.VMEM((2, WIDE, 16, NR), bf16),
            pltpu.VMEM((VIEWS, NH, NR), f32),
            pltpu.VMEM((VIEWS, NH, NR), f32),
            pltpu.VMEM((VIEWS, NH, NR), bf16),
            pltpu.VMEM((VIEWS, NH, NR), bf16),
            pltpu.VMEM((LAYERS, VIEWS, 8, NB), f32),
            pltpu.VMEM((ROWS, 8, 128), f32),
            dma((5,)), dma((2,)), dma((2, WIDE)), dma((2,)), dma, dma, dma((2,)), dma((ROWS,)), dma((ROWS,)),
        ],
        compiler_params=pltpu.CompilerParams(
            collective_id=0, has_side_effects=True, vmem_limit_bytes=48 * 1024 * 1024
        ),
    )(cotangent, amplitude, view_phase, jnp.swapaxes(layer_block, 1, 2), layer_phase.T, fourier_table())
    return grad_amp, grad_phase, grad_layers.T


def solution(mesh):
    in_specs = (
        P(None, "wide", "rows"),
        P("wide", None, "rows"),
        P("wide", None, "rows"),
        P("wide", None, "rows"),
        P(None, "wide"),
    )
    out_specs = (P("wide", None, "rows"), P("wide", None, "rows"), P(None, "wide"))
    return jax.shard_map(shards, mesh=mesh, in_specs=in_specs, out_specs=out_specs, check_vma=False)
```

time: 168 us -> 109 us (0.65)
  Pallas kernels: 0 us -> 99.1 us
  waiting for transfers between devices: 63.2 us -> 0 us
  blocking collectives: 43.1 us -> 0 us
  other arithmetic: 20.9 us -> 0 us
  starting transfers between devices: 19.9 us -> 0 us
  matrix products: 5.78 us -> 0 us
  local copies, waits for them, and re-layouts: 13.9 us -> 8.84 us
    pallas_call x0 -> x1, Pallas kernels: none -> 99.1 us  [shards(): pl.pallas_call(kernel, out_shape=(jax.ShapeDtypeStruct((VIEWS, NH, NR), b...]
    all_to_all x1 -> x0, waiting for transfers between devices: 62 us -> none  [shards(): lax.all_to_all(spectra, 'wide', split_axis=1, concat_axis=2, tiled=True)]
    psum x1 -> x0, blocking collectives: 43.1 us -> none  [shards(): total = lax.psum(table_part, 'rows')]
    all_to_all x1 -> x0, starting transfers between devices: 17.7 us -> none  [shards(): lax.all_to_all(spectra, 'wide', split_axis=1, concat_axis=2, tiled=True)]
    reduce_sum x1 -> x0, other arithmetic: 10.1 us -> none  [view_gradients(): jnp.sum(jnp.where(layers_rows == level, phase_term, 0.0), (1, 2))]
    cos x1 -> x0, other arithmetic: 7.96 us -> none  [view_gradients(): cosine = jnp.cos(angles)]
    dot_general x2 -> x0, matrix products: 5.78 us -> none  [half_product(): jnp.einsum('pkqn,qhnr->pkhr', table_half, frames, precision=lax.Precision...]
    convert_element_type x3 -> x0, local copies, waits for them, and re-layouts: 5.66 us -> none  [the longest x1 2.36 us: shards(): spectra = spectra.astype(jnp.bfloat16)]
  transfers between devices with their start and end apart: 2 -> 0, of which waited for: 2 -> 0; matrix products, arithmetic and copies ran while one was open for 9% -> 0% of each run, Pallas kernels for 0% -> 0%
where the time goes in v1:
time: 109 us
  Pallas kernels  99.1 us (91%)
  local copies, waits for them, and re-layouts  8.84 us (8%)
    pallas_call x1, Pallas kernels, shards(): pl.pallas_call(kernel, out_shape=(jax.ShapeDtypeStruct((VIEWS, NH, NR), b...  99.1 us
    unnamed x15, local copies, waits for them, and re-layouts  8.84 us

profile of v1, /device:TPU:6, one launch (start us, length us, event | category | flops | bytes accessed | tf_op | source)
XLA Modules:
  0.0 108.6 jit_solution(17516528254251941476)
XLA Ops:
  0.6 0.0 copy-start
  0.6 1.4 %copy-done = f32[2,512,384]{2,1,0:T(8,128)S(1)} copy-done((f32[2,512,384]{2,1,0:T(8,128)S(1)}, f32[2,512,384]{2,1,0:T(8,128)}, u32[]{:S(2)}) %copy-start) | copy-done | bytes 1572888
  2.0 0.0 copy-start.1
  2.0 1.2 %copy-done.1 = f32[512,512]{1,0:T(8,128)S(1)} copy-done((f32[512,512]{1,0:T(8,128)S(1)}, f32[512,512]{1,0:T(8,128)}, u32[]{:S(2)}) %copy-start.1) | copy-done | bytes 1048600
  3.3 0.0 copy-start.2
  3.3 1.1 %copy-done.2 = bf16[4,256,384]{2,1,0:T(8,128)(2,1)S(1)} copy-done((bf16[4,256,384]{2,1,0:T(8,128)(2,1)S(1)}, bf16[4,256,384]{2,1,0:T(8,128)(2,1)}, u32[]{:S(2)}) %copy-start.2) | copy-done | bytes 786456
  4.4 0.0 copy-start.3
  4.4 1.1 %copy-done.3 = bf16[4,256,384]{2,1,0:T(8,128)(2,1)S(1)} copy-done((bf16[4,256,384]{2,1,0:T(8,128)(2,1)S(1)}, bf16[4,256,384]{2,1,0:T(8,128)(2,1)}, u32[]{:S(2)}) %copy-start.3) | copy-done | bytes 786456
  5.5 0.0 copy-start.4
  5.5 0.9 copy-done.4
  6.5 0.0 copy-start.5
  6.5 0.7 copy-done.5
  7.1 99.1 %shard_map.85 = (bf16[4,256,384]{2,1,0:T(8,128)(2,1)S(1)}, bf16[4,256,384]{2,1,0:T(8,128)(2,1)S(1)}, f32[4,8]{1,0:T(4,128)S(1)}) custom-call(f32[2,512,384]{2,1,0:T(8,128)S(1)} %copy-done, bf16[4,256,384]{2,1,0:T(8,128)(2,1)S(1)} %copy-done.2, bf16[4,256,384]{2,1,0:T(8,128)(2,1)S(1)} %copy-done.3, s32[4,48,256]{2,1,0:T(8,128)S(1)} %bitcast.3, ...), custom_call_target="tpu_custom_call" | custom-call | tf_op jit(solution)/shard_map/pallas_call | solution.py:291
  106.3 0.9 copy.12
  107.1 0.9 copy.13
  108.0 0.6 copy.14
Async XLA Ops:
  0.6 1.4 %copy-start = (f32[2,512,384]{2,1,0:T(8,128)S(1)}, f32[2,512,384]{2,1,0:T(8,128)}, u32[]{:S(2)}) copy-start(f32[2,512,384]{2,1,0:T(8,128)} %cot_hbm.1) | copy-start | bytes 4718596
  2.0 1.2 %copy-start.1 = (f32[512,512]{1,0:T(8,128)S(1)}, f32[512,512]{1,0:T(8,128)}, u32[]{:S(2)}) copy-start(f32[512,512]{1,0:T(8,128)} %constant.2.clone.fourier_hbm) | copy-start | bytes 3145732
  3.3 1.1 %copy-start.2 = (bf16[4,256,384]{2,1,0:T(8,128)(2,1)S(1)}, bf16[4,256,384]{2,1,0:T(8,128)(2,1)}, u32[]{:S(2)}) copy-start(bf16[4,256,384]{2,1,0:T(8,128)(2,1)} %amp_hbm.1) | copy-start | bytes 2359300
  4.4 1.1 %copy-start.3 = (bf16[4,256,384]{2,1,0:T(8,128)(2,1)S(1)}, bf16[4,256,384]{2,1,0:T(8,128)(2,1)}, u32[]{:S(2)}) copy-start(bf16[4,256,384]{2,1,0:T(8,128)(2,1)} %phase_hbm.1) | copy-start | bytes 2359300
  5.5 0.9 copy-start.4
  6.5 0.7 copy-start.5

commit v2 on v1

--- a/solution.py
+++ b/solution.py
@@ -23,6 +23,14 @@
 NH = 256
 GROUP = 4
 GROUPS = WIDE // GROUP
+PLANE = 8
+PLANES = WIDE // PLANE
+ALONG = 4
+VISITS = (
+    (4, 5, 6, 7, 1, 2, 3, 0), (4, 5, 6, 0, 7, 2, 3, 1), (0, 1, 3, 4, 2, 5, 6, 7), (0, 1, 2, 3, 4, 5, 6, 7),
+    (0, 7, 1, 6, 2, 5, 3, 4), (0, 7, 2, 6, 1, 4, 3, 5), (1, 7, 0, 5, 3, 4, 2, 6), (1, 6, 0, 5, 3, 4, 2, 7),
+)
+ARRIVALS = tuple(tuple(sorted(range(PLANES), key=lambda s: VISITS[s].index(d) // 2)) for d in range(PLANES))
 COS = (0.999999989, -0.499999891, 0.0416664892, -0.00138878035, 2.47698825e-05, -2.70790202e-07, 1.72450525e-09)
 SIN = (0.999999999, -0.166666659, 0.00833332129, -0.000198405341, 2.75358492e-06, -2.47288044e-08, 1.36130722e-10)
 
@@ -73,74 +81,134 @@
     return jnp.dot(a, b, preferred_element_type=jnp.float32)
 
 
+def packed(orders, plane):
+    code = jnp.int32(0)
+    for index, order in enumerate(orders):
+        code = jnp.where(plane == index, sum(entry << (3 * i) for i, entry in enumerate(order)), code)
+    return code
+
+
+def entry_of(code, i):
+    return (code >> (3 * i)) & 7
+
+
 def kernel(
     cot_hbm, amp_hbm, phase_hbm, layer_hbm, table_ref, fourier_hbm,
     grad_amp_hbm, grad_phase_hbm, grad_layers_ref,
-    cot, amp, phase, layer_in, fourier, layer, thigh, tlow, spread, gather, order,
+    cot, amp, phase, layer_in, fourier, layer, spread, gather, order,
     xhigh, xlow, stage, recv, cosines, sines, grad_amp, grad_phase, sums, partial,
-    load_sem, send_sem, recv_sem, own_sem, halo_send, halo_recv, out_sem, row_send, row_recv,
+    load_sem, fourier_sem, send_sem, recv_sem, halo_send, halo_recv, out_sem, row_send, row_recv,
+    wide_sem, rows_sem,
 ):
     me = lax.axis_index("wide")
     row = lax.axis_index("rows")
+    plane, spot = me // PLANE, lax.rem(me, PLANE)
+    upper, along = row // ALONG, lax.rem(row, ALONG)
+
+    def greet(semaphore, **target):
+        pl.semaphore_signal(semaphore, inc=1, device_id=target, device_id_type=MESH)
+
+    def beside(n):
+        return plane * PLANE + lax.rem(spot + n, PLANE)
 
     barrier = pltpu.get_barrier_semaphore()
-
-    def greet_wide(n, carry):
-        other = lax.rem(me + n, WIDE)
-        pl.semaphore_signal(barrier, inc=1, device_id={"wide": other}, device_id_type=MESH)
-        return carry
-
-    lax.fori_loop(1, WIDE, greet_wide, 0)
-    for n in range(1, ROWS):
-        pl.semaphore_signal(barrier, inc=1, device_id={"rows": lax.rem(row + n, ROWS)}, device_id_type=MESH)
-
+    for n in range(1, PLANES):
+        greet(barrier, wide=lax.rem(plane + n, PLANES) * PLANE + spot)
+    for n in range(1, PLANE):
+        greet(barrier, wide=beside(n))
+    for n in range(1, ALONG):
+        greet(barrier, rows=upper * ALONG + lax.rem(along + n, ALONG))
+
+    @pl.when(upper == 0)
+    def _():
+        for n in range(ALONG):
+            greet(barrier, rows=ALONG + n)
+
+    visits = packed(VISITS, plane)
+    arrivals = packed(ARRIVALS, plane)
+
+    early = pl.ds(0, (HOGELS - 1) * HALF)
+    late = pl.ds((HOGELS - 1) * HALF, HALF)
+    cot_loads = [
+        pltpu.make_async_copy(cot_hbm.at[q, part], cot.at[q, part], load_sem.at[2 * i + q])
+        for i, part in enumerate((early, late))
+        for q in range(2)
+    ]
     loads = [
-        pltpu.make_async_copy(source, target, load_sem.at[i])
-        for i, (source, target) in enumerate(
-            (
-                (cot_hbm, cot), (fourier_hbm, fourier), (amp_hbm, amp), (phase_hbm, phase), (layer_hbm, layer_in),
-            )
-        )
+        pltpu.make_async_copy(source, target, load_sem.at[4 + i])
+        for i, (source, target) in enumerate(((amp_hbm, amp), (phase_hbm, phase), (layer_hbm, layer_in)))
     ]
+
+    def rows_of(there):
+        return pl.ds(pl.multiple_of(there * 64, 64), 64)
+
+    def fourier_load(i):
+        rows = rows_of(entry_of(visits, i))
+        return pltpu.make_async_copy(fourier_hbm.at[rows], fourier.at[rows], fourier_sem.at[i])
+
+    for load in cot_loads[:2]:
+        load.start()
+    for i in range(2):
+        fourier_load(i).start()
+    for load in cot_loads[2:]:
+        load.start()
+    for i in range(2, PLANES):
+        fourier_load(i).start()
     for load in loads:
         load.start()
-    loads[0].wait()
-    high, low = halves(cot[...])
-    xhigh[:, : HOGELS * HALF, :] = high
-    xlow[...] = low
-    loads[1].wait()
-    thigh[...], tlow[...] = halves(fourier[...])
-
-    def transform(hogel):
+
+    def ready(part, copies):
+        for copy in copies:
+            copy.wait()
+        high, low = halves(cot[:, part, :])
+        xhigh[:, part, :] = high
+        xlow[:, part, :] = low
+
+    def transform(there, hogel):
+        thigh, tlow = halves(fourier[rows_of(there), :])
+        first, last = hogel * HALF, hogel * HALF + HOG
         total = None
         for q in range(2):
-            columns = pl.ds(q * HOG, HOG)
-            upper = xhigh[q, hogel * HALF : hogel * HALF + HOG, :]
-            terms = [dot(thigh[:, columns], upper), dot(tlow[:, columns], upper)]
-            if hogel < HOGELS - 1:
-                terms.append(dot(thigh[:, columns], xlow[q, hogel * HALF : hogel * HALF + HOG, :]))
-            else:
-                terms.append(dot(thigh[:, q * HOG : q * HOG + HALF], xlow[q, hogel * HALF :, :]))
+            columns = slice(q * HOG, q * HOG + HOG)
+            terms = [dot(thigh[:, columns], xhigh[q, first:last, :]), dot(tlow[:, columns], xhigh[q, first:last, :])]
+            known = min(last, HOGELS * HALF)
+            terms.append(dot(thigh[:, q * HOG : q * HOG + known - first], xlow[q, first:known, :]))
             for term in terms:
                 total = term if total is None else total + term
-        return total.reshape(WIDE, 8, NR)
-
-    def send(half, n):
-        other = lax.rem(me + n, WIDE)
+        return total.reshape(PLANE, 8, NR)
+
+    def send(half, other):
         return pltpu.make_async_remote_copy(
             src_ref=stage.at[half, other], dst_ref=recv.at[half, me], send_sem=send_sem.at[half],
-            recv_sem=recv_sem.at[half, me], device_id={"wide": other}, device_id_type=MESH,
+            recv_sem=recv_sem.at[half, me // GROUP], device_id={"wide": other}, device_id_type=MESH,
         )
 
     def keep(half):
-        return pltpu.make_async_copy(stage.at[half, me], recv.at[half, me], own_sem.at[half])
-
-    def each_send(half, act):
+        return pltpu.make_async_copy(stage.at[half, me], recv.at[half, me], recv_sem.at[half, me // GROUP])
+
+    def prepare(half, quarter):
+        for side in range(2):
+            there = entry_of(visits, 2 * quarter + side)
+            both = [transform(there, 2 * half + hogel) for hogel in range(2)]
+            chunk = pl.ds(pl.multiple_of(there * PLANE, PLANE), PLANE)
+            stage[half, chunk] = jnp.concatenate(both, 1).astype(jnp.bfloat16)
+
+    def dispatch(half, quarter):
         def step(n, carry):
-            act(send(half, n))
+            there = entry_of(visits, 2 * quarter + lax.rem(n, 2))
+            other = there * PLANE + lax.rem(spot + n // 2, PLANE)
+
+            @pl.when(other != me)
+            def _():
+                send(half, other).start()
+
+            @pl.when(other == me)
+            def _():
+                keep(half).start()
+
             return carry
 
-        lax.fori_loop(1, WIDE, step, 0)
+        lax.fori_loop(0, 2 * PLANE, step, 0)
 
     halo = pltpu.make_async_remote_copy(
         src_ref=xhigh.at[:, pl.ds(0, HALF)], dst_ref=xhigh.at[:, pl.ds(HOGELS * HALF, HALF)],
@@ -148,16 +216,28 @@
         device_id={"wide": lax.rem(me + WIDE - 1, WIDE)}, device_id_type=MESH,
     )
 
-    stage[0] = jnp.concatenate([transform(0), transform(1)], 1).astype(jnp.bfloat16)
-    pl.semaphore_wait(barrier, WIDE - 1 + ROWS - 1)
+    ready(early, cot_loads[:2])
+    for i in range(2):
+        fourier_load(i).wait()
+    prepare(0, 0)
+
+    pl.semaphore_wait(barrier, PLANES + PLANE + ALONG - 3 + ALONG * upper)
+    for n in range(1, PLANE):
+        greet(wide_sem, wide=beside(n))
+
+    @pl.when(upper == 1)
+    def _():
+        for n in range(ALONG):
+            greet(rows_sem, rows=n)
+
+    pl.semaphore_wait(wide_sem, PLANE - 1)
 
     @pl.when(me > 0)
     def _():
         halo.start()
 
-    each_send(0, lambda copy: copy.start())
-    keep(0).start()
-    second = transform(2)
+    dispatch(0, 0)
+    ready(late, cot_loads[2:])
 
     @pl.when(me < WIDE - 1)
     def _():
@@ -167,11 +247,20 @@
     def _():
         xhigh[:, pl.ds(HOGELS * HALF, HALF), :] = jnp.zeros((2, HALF, NR), jnp.bfloat16)
 
-    stage[1] = jnp.concatenate([second, transform(3)], 1).astype(jnp.bfloat16)
-    each_send(1, lambda copy: copy.start())
-    keep(1).start()
-
-    for load in loads[2:]:
+    prepare(1, 0)
+    dispatch(1, 0)
+
+    def quarters(quarter, carry):
+        for half in range(2):
+            prepare(half, quarter)
+            dispatch(half, quarter)
+        return carry
+
+    for i in range(2, PLANES):
+        fourier_load(i).wait()
+    lax.fori_loop(1, PLANES // 2, quarters, 0)
+
+    for load in loads:
         load.wait()
     sums[...] = jnp.zeros_like(sums)
     order[...] = gather_order()
@@ -213,21 +302,12 @@
             for i, (source, target) in enumerate(((grad_amp, grad_amp_hbm), (grad_phase, grad_phase_hbm)))
         ]
 
-    keep(0).wait()
-    keep(1).wait()
-
     def gradients(n, carry):
-        group = lax.rem(me // GROUP + GROUPS - n, GROUPS)
+        group = 2 * entry_of(arrivals, n // 2) + lax.rem(n, 2)
         here = pl.ds(pl.multiple_of(group * 16, 16), 16)
-        for source in range(GROUP):
-            index = group * GROUP + source
-
-            @pl.when(index != me)
-            def _():
-                for half in range(2):
-                    landed = recv.at[half, index]
-                    pltpu.make_async_copy(landed, landed, recv_sem.at[half, index]).wait()
-
+        for half in range(2):
+            landed = recv.at[half, pl.ds(group * GROUP, GROUP)]
+            pltpu.make_async_copy(landed, landed, recv_sem.at[half, group]).wait()
         came = recv[:, pl.ds(group * GROUP, GROUP), :, :].reshape(2 * GROUP * 16, NR)
         ordered = dot(order[...], came)
         real = ordered[:64].reshape(VIEWS, 16, NR)
@@ -256,6 +336,11 @@
         lane = jnp.concatenate([lane, jnp.zeros((8 - VIEWS, 1), jnp.float32)], 0)
         own = jnp.where(level_of == l, lane, own)
     partial[0] = own
+
+    @pl.when(upper == 0)
+    def _():
+        pl.semaphore_wait(rows_sem, ALONG)
+
     for n in range(1, ROWS):
         pltpu.make_async_remote_copy(
             src_ref=partial.at[0], dst_ref=partial.at[n], send_sem=row_send.at[n], recv_sem=row_recv.at[n],
@@ -263,7 +348,8 @@
         ).start()
 
     for half in range(2):
-        each_send(half, lambda copy: copy.wait_send())
+        gone = stage.at[half, pl.ds(0, WIDE - 1)]
+        pltpu.make_async_copy(gone, gone, send_sem.at[half]).wait()
 
     @pl.when(me > 0)
     def _():
@@ -284,11 +370,27 @@
         copy.wait()
 
 
+def hand_over(amp_in, phase_in, layers_in, amp_out, phase_out, layers_out, amp, phase, layers, in_sem, out_sem):
+    pieces = [(layers_in, layers, layers_out)]
+    for view in range(VIEWS):
+        pieces.append((amp_in.at[view], amp.at[view], amp_out.at[view]))
+        pieces.append((phase_in.at[view], phase.at[view], phase_out.at[view]))
+    arrivals = [pltpu.make_async_copy(p[0], p[1], in_sem.at[i]) for i, p in enumerate(pieces)]
+    departures = [pltpu.make_async_copy(p[1], p[2], out_sem.at[i]) for i, p in enumerate(pieces)]
+    for copy in arrivals:
+        copy.start()
+    for arrival, departure in zip(arrivals, departures):
+        arrival.wait()
+        departure.start()
+    for copy in departures:
+        copy.wait()
+
+
 def shards(cotangent, amplitude, view_phase, layer_block, layer_phase):
     anywhere = pl.BlockSpec(memory_space=pl.ANY)
     bf16, f32 = jnp.bfloat16, jnp.float32
     dma = pltpu.SemaphoreType.DMA
-    grad_amp, grad_phase, grad_layers = pl.pallas_call(
+    grad_amp, grad_phase, grad_layers = grads = pl.pallas_call(
         kernel,
         out_shape=(
             jax.ShapeDtypeStruct((VIEWS, NH, NR), bf16),
@@ -304,8 +406,6 @@
             pltpu.VMEM((VIEWS, NB, NH), jnp.int32),
             pltpu.VMEM((2 * HOG, 2 * HOG), f32),
             pltpu.VMEM((VIEWS, NH, NB), f32),
-            pltpu.VMEM((2 * HOG, 2 * HOG), bf16),
-            pltpu.VMEM((2 * HOG, 2 * HOG), bf16),
             pltpu.VMEM((NB, NR), bf16),
             pltpu.VMEM((NR, NB), bf16),
             pltpu.VMEM((128, 128), bf16),
@@ -319,12 +419,21 @@
             pltpu.VMEM((VIEWS, NH, NR), bf16),
             pltpu.VMEM((LAYERS, VIEWS, 8, NB), f32),
             pltpu.VMEM((ROWS, 8, 128), f32),
-            dma((5,)), dma((2,)), dma((2, WIDE)), dma((2,)), dma, dma, dma((2,)), dma((ROWS,)), dma((ROWS,)),
+            dma((7,)), dma((PLANES,)), dma((2,)), dma((2, GROUPS)), dma, dma, dma((2,)), dma((ROWS,)), dma((ROWS,)),
+            pltpu.SemaphoreType.REGULAR, pltpu.SemaphoreType.REGULAR,
         ],
         compiler_params=pltpu.CompilerParams(
-            collective_id=0, has_side_effects=True, vmem_limit_bytes=48 * 1024 * 1024
+            collective_id=0, has_side_effects=True, vmem_limit_bytes=62 * 1024 * 1024
         ),
     )(cotangent, amplitude, view_phase, jnp.swapaxes(layer_block, 1, 2), layer_phase.T, fourier_table())
+    grad_amp, grad_phase, grad_layers = pl.pallas_call(
+        hand_over,
+        out_shape=tuple(jax.ShapeDtypeStruct(g.shape, g.dtype) for g in grads),
+        in_specs=[anywhere] * 3,
+        out_specs=(anywhere,) * 3,
+        scratch_shapes=[pltpu.VMEM(g.shape, g.dtype) for g in grads] + [dma((2 * VIEWS + 1,))] * 2,
+        compiler_params=pltpu.CompilerParams(vmem_limit_bytes=62 * 1024 * 1024),
+    )(*grads)
     return grad_amp, grad_phase, grad_layers.T
 
 

time: 109 us -> 101 us (0.927)
  the two profiles are of different devices: /device:TPU:6 before, /device:TPU:102 now
where the time goes in v2:
time: 101 us
  Pallas kernels  101 us (100%)
    pallas_call x1, Pallas kernels, shards(): pl.pallas_call(kernel, out_shape=(jax.ShapeDtypeStruct((VIEWS, NH, NR), b...  98.2 us
    pallas_call x1, Pallas kernels, shards(): pl.pallas_call(hand_over, out_shape=tuple((jax.ShapeDtypeStruct(g.shape,...  2.31 us

profile of v2, /device:TPU:102, one launch (start us, length us, event | category | flops | bytes accessed | tf_op | source)
XLA Modules:
  0.0 101.2 jit_solution(3472352010369081110)
XLA Ops:
  0.6 98.2 %shard_map.85 = (bf16[4,256,384]{2,1,0:T(8,128)(2,1)}, bf16[4,256,384]{2,1,0:T(8,128)(2,1)}, f32[4,8]{1,0:T(4,128)}) custom-call(f32[2,512,384]{2,1,0:T(8,128)} %cot_hbm.1, bf16[4,256,384]{2,1,0:T(8,128)(2,1)} %amp_hbm.1, bf16[4,256,384]{2,1,0:T(8,128)(2,1)} %phase_hbm.1, s32[4,48,256]{2,1,0:T(8,128)} %bitcast.3, f32[4,8]{1,0:T(4,128)} %bitcast.4, ...), custom_call_target="tpu_custom_call" | custom-call | tf_op jit(solution)/shard_map/pallas_call | solution.py:393
  98.9 2.3 %shard_map.86 = (bf16[4,256,384]{2,1,0:T(8,128)(2,1)}, bf16[4,256,384]{2,1,0:T(8,128)(2,1)}, f32[4,8]{1,0:T(4,128)}) custom-call(bf16[4,256,384]{2,1,0:T(8,128)(2,1)} %get-tuple-element.9.amp_in, bf16[4,256,384]{2,1,0:T(8,128)(2,1)} %get-tuple-element.10.phase_in, f32[4,8]{1,0:T(4,128)} %get-tuple-element.11.layers_in), custom_call_target="tpu_custom_call" | custom-call | tf_op jit(solution)/shard_map/pallas_call | solution.py:429

commit v3 on v2

--- a/solution.py
+++ b/solution.py
@@ -28,9 +28,14 @@
 ALONG = 4
 VISITS = (
     (4, 5, 6, 7, 1, 2, 3, 0), (4, 5, 6, 0, 7, 2, 3, 1), (0, 1, 3, 4, 2, 5, 6, 7), (0, 1, 2, 3, 4, 5, 6, 7),
-    (0, 7, 1, 6, 2, 5, 3, 4), (0, 7, 2, 6, 1, 4, 3, 5), (1, 7, 0, 5, 3, 4, 2, 6), (1, 6, 0, 5, 3, 4, 2, 7),
+    (0, 7, 1, 6, 2, 5, 3, 4), (0, 7, 2, 6, 1, 4, 3, 5), (1, 7, 0, 5, 3, 4, 2, 6), (0, 6, 1, 5, 3, 4, 2, 7),
+    (4, 5, 6, 7, 1, 2, 3, 0), (4, 5, 6, 0, 7, 2, 3, 1), (0, 1, 3, 4, 2, 5, 6, 7), (0, 1, 2, 3, 4, 5, 6, 7),
+    (0, 7, 1, 6, 2, 5, 3, 4), (0, 7, 2, 6, 1, 4, 3, 5), (1, 7, 0, 5, 3, 4, 2, 6), (3, 0, 1, 6, 5, 4, 2, 7),
 )
-ARRIVALS = tuple(tuple(sorted(range(PLANES), key=lambda s: VISITS[s].index(d) // 2)) for d in range(PLANES))
+LAST, UP, DOWN = PLANES - 1, 4, 3
+ARRIVALS = tuple(
+    tuple(sorted(range(PLANES), key=lambda s: VISITS[half + s].index(d) // 2)) for half in (0, PLANES) for d in range(PLANES)
+)
 COS = (0.999999989, -0.499999891, 0.0416664892, -0.00138878035, 2.47698825e-05, -2.70790202e-07, 1.72450525e-09)
 SIN = (0.999999999, -0.166666659, 0.00833332129, -0.000198405341, 2.75358492e-06, -2.47288044e-08, 1.36130722e-10)
 
@@ -81,10 +86,10 @@
     return jnp.dot(a, b, preferred_element_type=jnp.float32)
 
 
-def packed(orders, plane):
+def packed(orders, which):
     code = jnp.int32(0)
     for index, order in enumerate(orders):
-        code = jnp.where(plane == index, sum(entry << (3 * i) for i, entry in enumerate(order)), code)
+        code = jnp.where(which == index, sum(entry << (3 * i) for i, entry in enumerate(order)), code)
     return code
 
 
@@ -93,12 +98,12 @@
 
 
 def kernel(
-    cot_hbm, amp_hbm, phase_hbm, layer_hbm, table_ref, fourier_hbm,
+    cot_hbm, amp_hbm, phase_hbm, layer_hbm, table_hbm, fourier_hbm,
     grad_amp_hbm, grad_phase_hbm, grad_layers_ref,
-    cot, amp, phase, layer_in, fourier, layer, spread, gather, order,
-    xhigh, xlow, stage, recv, cosines, sines, grad_amp, grad_phase, sums, partial,
+    cot, amp, phase, layer_in, table_ref, fourier, layer, spread, gather, order,
+    xhigh, xlow, stage, recv, lent, cosines, sines, grad_amp, grad_phase, sums, partial,
     load_sem, fourier_sem, send_sem, recv_sem, halo_send, halo_recv, out_sem, row_send, row_recv,
-    wide_sem, rows_sem,
+    lent_sem, passed_sem, wide_sem, rows_sem,
 ):
     me = lax.axis_index("wide")
     row = lax.axis_index("rows")
@@ -124,8 +129,18 @@
         for n in range(ALONG):
             greet(barrier, rows=ALONG + n)
 
-    visits = packed(VISITS, plane)
-    arrivals = packed(ARRIVALS, plane)
+    relays = (upper == 0) & (plane == UP)
+    relayed = (upper == 1) & (plane == LAST)
+    rising = (plane == LAST) | (plane == UP)
+    lender, borrower = jnp.where(rising, LAST, 0), jnp.where(rising, DOWN, UP)
+    through = jnp.where(rising, UP, DOWN)
+
+    @pl.when(relays)
+    def _():
+        greet(barrier, wide=lender * PLANE + spot, rows=ALONG + along)
+
+    visits = packed(VISITS, upper * PLANES + plane)
+    arrivals = packed(ARRIVALS, upper * PLANES + plane)
 
     early = pl.ds(0, (HOGELS - 1) * HALF)
     late = pl.ds((HOGELS - 1) * HALF, HALF)
@@ -136,7 +151,9 @@
     ]
     loads = [
         pltpu.make_async_copy(source, target, load_sem.at[4 + i])
-        for i, (source, target) in enumerate(((amp_hbm, amp), (phase_hbm, phase), (layer_hbm, layer_in)))
+        for i, (source, target) in enumerate((
+            ((amp_hbm, amp), (phase_hbm, phase), (layer_hbm, layer_in), (table_hbm, table_ref))
+        ))
     ]
 
     def rows_of(there):
@@ -180,11 +197,11 @@
     def send(half, other):
         return pltpu.make_async_remote_copy(
             src_ref=stage.at[half, other], dst_ref=recv.at[half, me], send_sem=send_sem.at[half],
-            recv_sem=recv_sem.at[half, me // GROUP], device_id={"wide": other}, device_id_type=MESH,
+            recv_sem=recv_sem.at[half, plane], device_id={"wide": other}, device_id_type=MESH,
         )
 
     def keep(half):
-        return pltpu.make_async_copy(stage.at[half, me], recv.at[half, me], recv_sem.at[half, me // GROUP])
+        return pltpu.make_async_copy(stage.at[half, me], recv.at[half, me], recv_sem.at[half, plane])
 
     def prepare(half, quarter):
         for side in range(2):
@@ -193,12 +210,28 @@
             chunk = pl.ds(pl.multiple_of(there * PLANE, PLANE), PLANE)
             stage[half, chunk] = jnp.concatenate(both, 1).astype(jnp.bfloat16)
 
+    def lend(half):
+        return pltpu.make_async_remote_copy(
+            src_ref=stage.at[half, pl.ds(borrower * PLANE, PLANE)], dst_ref=lent.at[half], send_sem=send_sem.at[half],
+            recv_sem=lent_sem.at[half], device_id={"wide": through * PLANE + spot, "rows": along}, device_id_type=MESH,
+        )
+
+    def pass_on(half, n):
+        return pltpu.make_async_remote_copy(
+            src_ref=lent.at[half, n], dst_ref=recv.at[half, lender * PLANE + spot], send_sem=passed_sem.at[half],
+            recv_sem=recv_sem.at[half, lender], device_id={"wide": borrower * PLANE + n, "rows": ALONG + along}, device_id_type=MESH,
+        )
+
     def dispatch(half, quarter):
+        @pl.when(relayed & (quarter == 0) & (half == 1))
+        def _():
+            lend(half).start()
+
         def step(n, carry):
             there = entry_of(visits, 2 * quarter + lax.rem(n, 2))
             other = there * PLANE + lax.rem(spot + n // 2, PLANE)
 
-            @pl.when(other != me)
+            @pl.when((other != me) & ~(relayed & (there == borrower) & (half == 1)))
             def _():
                 send(half, other).start()
 
@@ -221,7 +254,7 @@
         fourier_load(i).wait()
     prepare(0, 0)
 
-    pl.semaphore_wait(barrier, PLANES + PLANE + ALONG - 3 + ALONG * upper)
+    pl.semaphore_wait(barrier, PLANES + PLANE + ALONG - 3 + ALONG * upper + relayed.astype(jnp.int32))
     for n in range(1, PLANE):
         greet(wide_sem, wide=beside(n))
 
@@ -295,39 +328,55 @@
 
     lax.fori_loop(0, GROUPS, angles, 0)
 
-    def finished(group):
-        here = pl.ds(pl.multiple_of(group * 16, 16), 16)
+    @pl.when(relays)
+    def _():
+        for half in (1,):
+            pltpu.make_async_copy(lent.at[half], lent.at[half], lent_sem.at[half]).wait()
+
+            def forward(n, carry):
+                pass_on(half, n).start()
+                return carry
+
+            lax.fori_loop(0, PLANE, forward, 0)
+
+    def finished(here):
         return [
             pltpu.make_async_copy(source.at[:, here], target.at[:, here], out_sem.at[i])
             for i, (source, target) in enumerate(((grad_amp, grad_amp_hbm), (grad_phase, grad_phase_hbm)))
         ]
 
     def gradients(n, carry):
-        group = 2 * entry_of(arrivals, n // 2) + lax.rem(n, 2)
-        here = pl.ds(pl.multiple_of(group * 16, 16), 16)
+        origin = entry_of(arrivals, n)
+        hogels = PLANE * HOGELS
+        here = pl.ds(pl.multiple_of(origin * hogels, hogels), hogels)
         for half in range(2):
-            landed = recv.at[half, pl.ds(group * GROUP, GROUP)]
-            pltpu.make_async_copy(landed, landed, recv_sem.at[half, group]).wait()
-        came = recv[:, pl.ds(group * GROUP, GROUP), :, :].reshape(2 * GROUP * 16, NR)
-        ordered = dot(order[...], came)
-        real = ordered[:64].reshape(VIEWS, 16, NR)
-        imag = ordered[64:].reshape(VIEWS, 16, NR)
+            landed = recv.at[half, pl.ds(origin * PLANE, PLANE)]
+            pltpu.make_async_copy(landed, landed, recv_sem.at[half, origin]).wait()
+        came = [
+            recv[:, pl.ds(origin * PLANE + first, GROUP), :, :].reshape(2 * GROUP * 16, NR) for first in (0, GROUP)
+        ]
+        ordered = dot(order[...], jnp.concatenate(came, 1))
+
+        def part(rows):
+            return jnp.concatenate([ordered[rows, i * NR : (i + 1) * NR].reshape(VIEWS, 16, NR) for i in range(2)], 1)
+
+        real, imag = part(slice(0, 64)), part(slice(64, 128))
         cosine = cosines[:, here, :]
         sine = sines[:, here, :]
+        term = amp[:, here, :].astype(jnp.float32) * (imag * cosine - real * sine)
+        flat = term.reshape(VIEWS * hogels, NR)
+        blocks = sum(dot(part, gather[...]) for part in halves(flat)).reshape(VIEWS, hogels, NB)
         grad_amp[:, here, :] = (real * cosine + imag * sine).astype(jnp.bfloat16)
-        term = amp[:, here, :].astype(jnp.float32) * (imag * cosine - real * sine)
         grad_phase[:, here, :] = term.astype(jnp.bfloat16)
-        for copy in finished(group):
+        for copy in finished(here):
             copy.start()
-        flat = term.reshape(VIEWS * 16, NR)
-        blocks = sum(dot(part, gather[...]) for part in halves(flat)).reshape(VIEWS, 16, NB)
         level = layer[:, here, :]
         for l in range(LAYERS):
             chosen = jnp.where(level == float(l), blocks, 0.0)
-            sums[l] += chosen[:, :8, :] + chosen[:, 8:, :]
+            sums[l] += jnp.sum(chosen.reshape(VIEWS, hogels // 8, 8, NB), axis=1)
         return carry
 
-    lax.fori_loop(0, GROUPS, gradients, 0)
+    lax.fori_loop(0, PLANES, gradients, 0)
 
     view_of, level_of = places((8, 128))
     own = jnp.zeros((8, 128), jnp.float32)
@@ -350,6 +399,11 @@
     for half in range(2):
         gone = stage.at[half, pl.ds(0, WIDE - 1)]
         pltpu.make_async_copy(gone, gone, send_sem.at[half]).wait()
+
+    @pl.when(relays)
+    def _():
+        for half in (1,):
+            pltpu.make_async_copy(lent.at[half], lent.at[half], passed_sem.at[half]).wait()
 
     @pl.when(me > 0)
     def _():
@@ -397,13 +451,14 @@
             jax.ShapeDtypeStruct((VIEWS, NH, NR), bf16),
             jax.ShapeDtypeStruct((VIEWS, LAYERS), f32),
         ),
-        in_specs=[anywhere] * 4 + [pl.BlockSpec(memory_space=pltpu.SMEM), anywhere],
+        in_specs=[anywhere] * 6,
         out_specs=(anywhere, anywhere, pl.BlockSpec(memory_space=pltpu.VMEM)),
         scratch_shapes=[
             pltpu.VMEM((2, HOGELS * HALF, NR), f32),
             pltpu.VMEM((VIEWS, NH, NR), bf16),
             pltpu.VMEM((VIEWS, NH, NR), bf16),
             pltpu.VMEM((VIEWS, NB, NH), jnp.int32),
+            pltpu.SMEM((VIEWS, LAYERS), f32),
             pltpu.VMEM((2 * HOG, 2 * HOG), f32),
             pltpu.VMEM((VIEWS, NH, NB), f32),
             pltpu.VMEM((NB, NR), bf16),
@@ -413,14 +468,15 @@
             pltpu.VMEM((2, HOGELS * HALF, NR), bf16),
             pltpu.VMEM((2, WIDE, 16, NR), bf16),
             pltpu.VMEM((2, WIDE, 16, NR), bf16),
+            pltpu.VMEM((2, PLANE, 16, NR), bf16),
             pltpu.VMEM((VIEWS, NH, NR), f32),
             pltpu.VMEM((VIEWS, NH, NR), f32),
             pltpu.VMEM((VIEWS, NH, NR), bf16),
             pltpu.VMEM((VIEWS, NH, NR), bf16),
             pltpu.VMEM((LAYERS, VIEWS, 8, NB), f32),
             pltpu.VMEM((ROWS, 8, 128), f32),
-            dma((7,)), dma((PLANES,)), dma((2,)), dma((2, GROUPS)), dma, dma, dma((2,)), dma((ROWS,)), dma((ROWS,)),
-            pltpu.SemaphoreType.REGULAR, pltpu.SemaphoreType.REGULAR,
+            dma((8,)), dma((PLANES,)), dma((2,)), dma((2, PLANES)), dma, dma, dma((2,)), dma((ROWS,)), dma((ROWS,)),
+            dma((2,)), dma((2,)), pltpu.SemaphoreType.REGULAR, pltpu.SemaphoreType.REGULAR,
         ],
         compiler_params=pltpu.CompilerParams(
             collective_id=0, has_side_effects=True, vmem_limit_bytes=62 * 1024 * 1024

time: 101 us -> 97.9 us (0.969)
  the two profiles are of different devices: /device:TPU:102 before, /device:TPU:6 now
where the time goes in v3:
time: 97.9 us; the launch traced here: 96.1 us
  Pallas kernels  95.5 us (98%)
    pallas_call x1, Pallas kernels, shards(): pl.pallas_call(kernel, out_shape=(jax.ShapeDtypeStruct((VIEWS, NH, NR), b...  93.1 us
    pallas_call x1, Pallas kernels, shards(): pl.pallas_call(hand_over, out_shape=tuple((jax.ShapeDtypeStruct(g.shape,...  2.31 us

profile of v3, /device:TPU:6, one launch (start us, length us, event | category | flops | bytes accessed | tf_op | source)
XLA Modules:
  0.0 96.1 jit_solution(2142316383120240254)
XLA Ops:
  0.6 93.1 %shard_map.85 = (bf16[4,256,384]{2,1,0:T(8,128)(2,1)}, bf16[4,256,384]{2,1,0:T(8,128)(2,1)}, f32[4,8]{1,0:T(4,128)}) custom-call(f32[2,512,384]{2,1,0:T(8,128)} %cot_hbm.1, bf16[4,256,384]{2,1,0:T(8,128)(2,1)} %amp_hbm.1, bf16[4,256,384]{2,1,0:T(8,128)(2,1)} %phase_hbm.1, s32[4,48,256]{2,1,0:T(8,128)} %bitcast.3, f32[4,8]{1,0:T(4,128)} %bitcast.4, ...), custom_call_target="tpu_custom_call" | custom-call | tf_op jit(solution)/shard_map/pallas_call | solution.py:447
  93.8 2.3 %shard_map.86 = (bf16[4,256,384]{2,1,0:T(8,128)(2,1)}, bf16[4,256,384]{2,1,0:T(8,128)(2,1)}, f32[4,8]{1,0:T(4,128)}) custom-call(bf16[4,256,384]{2,1,0:T(8,128)(2,1)} %get-tuple-element.9.amp_in, bf16[4,256,384]{2,1,0:T(8,128)(2,1)} %get-tuple-element.10.phase_in, f32[4,8]{1,0:T(4,128)} %get-tuple-element.11.layers_in), custom_call_target="tpu_custom_call" | custom-call | tf_op jit(solution)/shard_map/pallas_call | solution.py:485

commit v4 on v3

--- a/solution.py
+++ b/solution.py
@@ -99,10 +99,10 @@
 
 def kernel(
     cot_hbm, amp_hbm, phase_hbm, layer_hbm, table_hbm, fourier_hbm,
-    grad_amp_hbm, grad_phase_hbm, grad_layers_ref,
+    grad_amp, grad_phase, grad_layers_ref,
     cot, amp, phase, layer_in, table_ref, fourier, layer, spread, gather, order,
-    xhigh, xlow, stage, recv, lent, cosines, sines, grad_amp, grad_phase, sums, partial,
-    load_sem, fourier_sem, send_sem, recv_sem, halo_send, halo_recv, out_sem, row_send, row_recv,
+    xhigh, xlow, stage, recv, lent, cosines, sines, sums, partial,
+    load_sem, fourier_sem, send_sem, recv_sem, halo_send, halo_recv, row_send, row_recv,
     lent_sem, passed_sem, wide_sem, rows_sem,
 ):
     me = lax.axis_index("wide")
@@ -339,12 +339,6 @@
 
             lax.fori_loop(0, PLANE, forward, 0)
 
-    def finished(here):
-        return [
-            pltpu.make_async_copy(source.at[:, here], target.at[:, here], out_sem.at[i])
-            for i, (source, target) in enumerate(((grad_amp, grad_amp_hbm), (grad_phase, grad_phase_hbm)))
-        ]
-
     def gradients(n, carry):
         origin = entry_of(arrivals, n)
         hogels = PLANE * HOGELS
@@ -368,8 +362,6 @@
         blocks = sum(dot(part, gather[...]) for part in halves(flat)).reshape(VIEWS, hogels, NB)
         grad_amp[:, here, :] = (real * cosine + imag * sine).astype(jnp.bfloat16)
         grad_phase[:, here, :] = term.astype(jnp.bfloat16)
-        for copy in finished(here):
-            copy.start()
         level = layer[:, here, :]
         for l in range(LAYERS):
             chosen = jnp.where(level == float(l), blocks, 0.0)
@@ -417,26 +409,15 @@
         pltpu.make_async_copy(partial.at[0], partial.at[0], row_send.at[n]).wait()
     grad_layers_ref[...] = (total * (1.0 / math.sqrt(NR * ROWS * NH)))[:VIEWS, :LAYERS]
 
-    for copy in [
-        pltpu.make_async_copy(grad_amp, grad_amp_hbm, out_sem.at[0]),
-        pltpu.make_async_copy(grad_phase, grad_phase_hbm, out_sem.at[1]),
-    ]:
-        copy.wait()
-
-
-def hand_over(amp_in, phase_in, layers_in, amp_out, phase_out, layers_out, amp, phase, layers, in_sem, out_sem):
-    pieces = [(layers_in, layers, layers_out)]
+
+def hand_over(amp_in, phase_in, layers_in, amp_out, phase_out, layers_out, sem):
+    copies = [pltpu.make_async_copy(layers_in, layers_out, sem.at[2 * VIEWS])]
     for view in range(VIEWS):
-        pieces.append((amp_in.at[view], amp.at[view], amp_out.at[view]))
-        pieces.append((phase_in.at[view], phase.at[view], phase_out.at[view]))
-    arrivals = [pltpu.make_async_copy(p[0], p[1], in_sem.at[i]) for i, p in enumerate(pieces)]
-    departures = [pltpu.make_async_copy(p[1], p[2], out_sem.at[i]) for i, p in enumerate(pieces)]
-    for copy in arrivals:
+        copies.append(pltpu.make_async_copy(amp_in.at[view], amp_out.at[view], sem.at[view]))
+        copies.append(pltpu.make_async_copy(phase_in.at[view], phase_out.at[view], sem.at[VIEWS + view]))
+    for copy in copies:
         copy.start()
-    for arrival, departure in zip(arrivals, departures):
-        arrival.wait()
-        departure.start()
-    for copy in departures:
+    for copy in copies:
         copy.wait()
 
 
@@ -447,12 +428,12 @@
     grad_amp, grad_phase, grad_layers = grads = pl.pallas_call(
         kernel,
         out_shape=(
-            jax.ShapeDtypeStruct((VIEWS, NH, NR), bf16),
-            jax.ShapeDtypeStruct((VIEWS, NH, NR), bf16),
-            jax.ShapeDtypeStruct((VIEWS, LAYERS), f32),
+            pltpu.VMEM((VIEWS, NH, NR), bf16),
+            pltpu.VMEM((VIEWS, NH, NR), bf16),
+            pltpu.VMEM((VIEWS, LAYERS), f32),
         ),
         in_specs=[anywhere] * 6,
-        out_specs=(anywhere, anywhere, pl.BlockSpec(memory_space=pltpu.VMEM)),
+        out_specs=(pl.BlockSpec(memory_space=pltpu.VMEM),) * 3,
         scratch_shapes=[
             pltpu.VMEM((2, HOGELS * HALF, NR), f32),
             pltpu.VMEM((VIEWS, NH, NR), bf16),
@@ -471,25 +452,22 @@
             pltpu.VMEM((2, PLANE, 16, NR), bf16),
             pltpu.VMEM((VIEWS, NH, NR), f32),
             pltpu.VMEM((VIEWS, NH, NR), f32),
-            pltpu.VMEM((VIEWS, NH, NR), bf16),
-            pltpu.VMEM((VIEWS, NH, NR), bf16),
             pltpu.VMEM((LAYERS, VIEWS, 8, NB), f32),
             pltpu.VMEM((ROWS, 8, 128), f32),
-            dma((8,)), dma((PLANES,)), dma((2,)), dma((2, PLANES)), dma, dma, dma((2,)), dma((ROWS,)), dma((ROWS,)),
+            dma((8,)), dma((PLANES,)), dma((2,)), dma((2, PLANES)), dma, dma, dma((ROWS,)), dma((ROWS,)),
             dma((2,)), dma((2,)), pltpu.SemaphoreType.REGULAR, pltpu.SemaphoreType.REGULAR,
         ],
         compiler_params=pltpu.CompilerParams(
-            collective_id=0, has_side_effects=True, vmem_limit_bytes=62 * 1024 * 1024
+            collective_id=0, has_side_effects=True, vmem_limit_bytes=61 * 1024 * 1024
         ),
     )(cotangent, amplitude, view_phase, jnp.swapaxes(layer_block, 1, 2), layer_phase.T, fourier_table())
     grad_amp, grad_phase, grad_layers = pl.pallas_call(
         hand_over,
         out_shape=tuple(jax.ShapeDtypeStruct(g.shape, g.dtype) for g in grads),
-        in_specs=[anywhere] * 3,
+        in_specs=[pl.BlockSpec(memory_space=pltpu.VMEM)] * 3,
         out_specs=(anywhere,) * 3,
-        scratch_shapes=[pltpu.VMEM(g.shape, g.dtype) for g in grads] + [dma((2 * VIEWS + 1,))] * 2,
-        compiler_params=pltpu.CompilerParams(vmem_limit_bytes=62 * 1024 * 1024),
-    )(*grads)
+        scratch_shapes=[dma((2 * VIEWS + 1,))],
+    )(*(pltpu.with_memory_space_constraint(g, pltpu.VMEM) for g in grads))
     return grad_amp, grad_phase, grad_layers.T
 
 

time: 97.9 us -> 96.2 us (0.983)
  Pallas kernels: 95.5 us -> 93.8 us
    pallas_call x1, Pallas kernels: 2.31 us -> 1.21 us  [shards(): pl.pallas_call(hand_over, out_shape=tuple((jax.ShapeDtypeStruct(g.shape,...]
where the time goes in v4:
time: 96.2 us; the launch traced here: 94.4 us
  Pallas kernels  93.8 us (98%)
    pallas_call x1, Pallas kernels, shards(): pl.pallas_call(kernel, out_shape=(pltpu.VMEM((VIEWS, NH, NR), bf16), pltp...  92.6 us

profile of v4, /device:TPU:6, one launch (start us, length us, event | category | flops | bytes accessed | tf_op | source)
XLA Modules:
  0.0 94.4 jit_solution(6529897463512352915)
XLA Ops:
  0.6 92.6 %shard_map.85 = (bf16[4,256,384]{2,1,0:T(8,128)(2,1)S(1)}, bf16[4,256,384]{2,1,0:T(8,128)(2,1)S(1)}, f32[4,8]{1,0:T(4,128)S(1)}) custom-call(f32[2,512,384]{2,1,0:T(8,128)} %cot_hbm.1, bf16[4,256,384]{2,1,0:T(8,128)(2,1)} %amp_hbm.1, bf16[4,256,384]{2,1,0:T(8,128)(2,1)} %phase_hbm.1, s32[4,48,256]{2,1,0:T(8,128)} %bitcast.3, f32[4,8]{1,0:T(4,128)} %bitcast.4, ...), custom_call_target="tpu_custom_call" | custom-call | tf_op jit(solution)/shard_map/pallas_call | solution.py:428
  93.2 1.2 %shard_map.86 = (bf16[4,256,384]{2,1,0:T(8,128)(2,1)}, bf16[4,256,384]{2,1,0:T(8,128)(2,1)}, f32[4,8]{1,0:T(4,128)}) custom-call(bf16[4,256,384]{2,1,0:T(8,128)(2,1)S(1)} %get-tuple-element.9.amp_in, bf16[4,256,384]{2,1,0:T(8,128)(2,1)S(1)} %get-tuple-element.10.phase_in, f32[4,8]{1,0:T(4,128)S(1)} %get-tuple-element.11.layers_in), custom_call_target="tpu_custom_call" | custom-call | tf_op jit(solution)/shard_map/pallas_call | solution.py:464

commit v5 on v4

--- a/solution.py
+++ b/solution.py
@@ -27,12 +27,25 @@
 PLANES = WIDE // PLANE
 ALONG = 4
 VISITS = (
-    (4, 5, 6, 7, 1, 2, 3, 0), (4, 5, 6, 0, 7, 2, 3, 1), (0, 1, 3, 4, 2, 5, 6, 7), (0, 1, 2, 3, 4, 5, 6, 7),
-    (0, 7, 1, 6, 2, 5, 3, 4), (0, 7, 2, 6, 1, 4, 3, 5), (1, 7, 0, 5, 3, 4, 2, 6), (0, 6, 1, 5, 3, 4, 2, 7),
-    (4, 5, 6, 7, 1, 2, 3, 0), (4, 5, 6, 0, 7, 2, 3, 1), (0, 1, 3, 4, 2, 5, 6, 7), (0, 1, 2, 3, 4, 5, 6, 7),
-    (0, 7, 1, 6, 2, 5, 3, 4), (0, 7, 2, 6, 1, 4, 3, 5), (1, 7, 0, 5, 3, 4, 2, 6), (3, 0, 1, 6, 5, 4, 2, 7),
+    (4, 5, 6, 7, 1, 2, 3, 0),
+    (4, 6, 7, 0, 5, 2, 3, 1),
+    (0, 1, 3, 4, 2, 7, 6, 5),
+    (0, 1, 2, 3, 4, 5, 6, 7),
+    (0, 7, 1, 6, 2, 5, 3, 4),
+    (0, 7, 2, 6, 1, 4, 3, 5),
+    (1, 7, 0, 5, 3, 4, 2, 6),
+    (0, 6, 1, 5, 3, 4, 2, 7),
+    (4, 5, 6, 7, 1, 2, 3, 0),
+    (4, 6, 7, 0, 5, 2, 3, 1),
+    (0, 1, 3, 4, 2, 7, 6, 5),
+    (0, 1, 2, 3, 4, 5, 6, 7),
+    (0, 7, 1, 6, 2, 5, 3, 4),
+    (0, 7, 2, 6, 1, 4, 3, 5),
+    (1, 7, 0, 5, 3, 4, 2, 6),
+    (3, 0, 1, 6, 5, 4, 2, 7),
 )
 LAST, UP, DOWN = PLANES - 1, 4, 3
+LENT = (1,)
 ARRIVALS = tuple(
     tuple(sorted(range(PLANES), key=lambda s: VISITS[half + s].index(d) // 2)) for half in (0, PLANES) for d in range(PLANES)
 )
@@ -222,8 +235,8 @@
             recv_sem=recv_sem.at[half, lender], device_id={"wide": borrower * PLANE + n, "rows": ALONG + along}, device_id_type=MESH,
         )
 
-    def dispatch(half, quarter):
-        @pl.when(relayed & (quarter == 0) & (half == 1))
+    def dispatch(half, quarter, first=0, last=2 * PLANE):
+        @pl.when(relayed & (quarter == 0) & (half in LENT) & (last > 2))
         def _():
             lend(half).start()
 
@@ -231,7 +244,7 @@
             there = entry_of(visits, 2 * quarter + lax.rem(n, 2))
             other = there * PLANE + lax.rem(spot + n // 2, PLANE)
 
-            @pl.when((other != me) & ~(relayed & (there == borrower) & (half == 1)))
+            @pl.when((other != me) & ~(relayed & (there == borrower) & (half in LENT)))
             def _():
                 send(half, other).start()
 
@@ -241,7 +254,7 @@
 
             return carry
 
-        lax.fori_loop(0, 2 * PLANE, step, 0)
+        lax.fori_loop(first, last, step, 0)
 
     halo = pltpu.make_async_remote_copy(
         src_ref=xhigh.at[:, pl.ds(0, HALF)], dst_ref=xhigh.at[:, pl.ds(HOGELS * HALF, HALF)],
@@ -258,6 +271,11 @@
     for n in range(1, PLANE):
         greet(wide_sem, wide=beside(n))
 
+    dispatch(0, 0, 0, 2)
+    for i in (2, 3):
+        fourier_load(i).wait()
+    prepare(0, 1)
+    dispatch(0, 1, 0, 2)
     @pl.when(upper == 1)
     def _():
         for n in range(ALONG):
@@ -269,7 +287,7 @@
     def _():
         halo.start()
 
-    dispatch(0, 0)
+    dispatch(0, 0, 2)
     ready(late, cot_loads[2:])
 
     @pl.when(me < WIDE - 1)
@@ -284,12 +302,16 @@
     dispatch(1, 0)
 
     def quarters(quarter, carry):
-        for half in range(2):
-            prepare(half, quarter)
-            dispatch(half, quarter)
+        @pl.when(quarter > 1)
+        def _():
+            prepare(0, quarter)
+
+        dispatch(0, quarter, jnp.where(quarter == 1, 2, 0))
+        prepare(1, quarter)
+        dispatch(1, quarter)
         return carry
 
-    for i in range(2, PLANES):
+    for i in range(4, PLANES):
         fourier_load(i).wait()
     lax.fori_loop(1, PLANES // 2, quarters, 0)
 
@@ -330,7 +352,7 @@
 
     @pl.when(relays)
     def _():
-        for half in (1,):
+        for half in LENT:
             pltpu.make_async_copy(lent.at[half], lent.at[half], lent_sem.at[half]).wait()
 
             def forward(n, carry):
@@ -394,7 +416,7 @@
 
     @pl.when(relays)
     def _():
-        for half in (1,):
+        for half in LENT:
             pltpu.make_async_copy(lent.at[half], lent.at[half], passed_sem.at[half]).wait()
 
     @pl.when(me > 0)

time: 96.2 us -> 94.1 us (0.978)
  Pallas kernels: 93.8 us -> 92.5 us
    pallas_call x1, Pallas kernels: 92.6 us -> 91.2 us  [shards(): pl.pallas_call(kernel, out_shape=(pltpu.VMEM((VIEWS, NH, NR), bf16), pltp...]
where the time goes in v5:
time: 94.1 us; the launch traced here: 93.1 us
  Pallas kernels  92.5 us (98%)
    pallas_call x1, Pallas kernels, shards(): pl.pallas_call(kernel, out_shape=(pltpu.VMEM((VIEWS, NH, NR), bf16), pltp...  91.2 us

profile of v5, /device:TPU:6, one launch (start us, length us, event | category | flops | bytes accessed | tf_op | source)
XLA Modules:
  0.0 93.1 jit_solution(7853981214055011707)
XLA Ops:
  0.6 91.2 %shard_map.85 = (bf16[4,256,384]{2,1,0:T(8,128)(2,1)S(1)}, bf16[4,256,384]{2,1,0:T(8,128)(2,1)S(1)}, f32[4,8]{1,0:T(4,128)S(1)}) custom-call(f32[2,512,384]{2,1,0:T(8,128)} %cot_hbm.1, bf16[4,256,384]{2,1,0:T(8,128)(2,1)} %amp_hbm.1, bf16[4,256,384]{2,1,0:T(8,128)(2,1)} %phase_hbm.1, s32[4,48,256]{2,1,0:T(8,128)} %bitcast.3, f32[4,8]{1,0:T(4,128)} %bitcast.4, ...), custom_call_target="tpu_custom_call" | custom-call | tf_op jit(solution)/shard_map/pallas_call | solution.py:450
  91.9 1.2 %shard_map.86 = (bf16[4,256,384]{2,1,0:T(8,128)(2,1)}, bf16[4,256,384]{2,1,0:T(8,128)(2,1)}, f32[4,8]{1,0:T(4,128)}) custom-call(bf16[4,256,384]{2,1,0:T(8,128)(2,1)S(1)} %get-tuple-element.9.amp_in, bf16[4,256,384]{2,1,0:T(8,128)(2,1)S(1)} %get-tuple-element.10.phase_in, f32[4,8]{1,0:T(4,128)S(1)} %get-tuple-element.11.layers_in), custom_call_target="tpu_custom_call" | custom-call | tf_op jit(solution)/shard_map/pallas_call | solution.py:486

commit v6 on v5

--- a/solution.py
+++ b/solution.py
@@ -404,7 +404,7 @@
     def _():
         pl.semaphore_wait(rows_sem, ALONG)
 
-    for n in range(1, ROWS):
+    for n in (4, 3, 5, 2, 6, 1, 7):
         pltpu.make_async_remote_copy(
             src_ref=partial.at[0], dst_ref=partial.at[n], send_sem=row_send.at[n], recv_sem=row_recv.at[n],
             device_id={"rows": lax.rem(row + n, ROWS)}, device_id_type=MESH,

time: 94.1 us -> 94.3 us (level)
  no operation moved by 1% of the time
where the time goes in v6:
time: 94.3 us; the launch traced here: 93.2 us
  Pallas kernels  92.6 us (98%)
    pallas_call x1, Pallas kernels, shards(): pl.pallas_call(kernel, out_shape=(pltpu.VMEM((VIEWS, NH, NR), bf16), pltp...  91.4 us

profile of v6, /device:TPU:6, one launch (start us, length us, event | category | flops | bytes accessed | tf_op | source)
XLA Modules:
  0.0 93.2 jit_solution(6700087045767628395)
XLA Ops:
  0.6 91.4 %shard_map.85 = (bf16[4,256,384]{2,1,0:T(8,128)(2,1)S(1)}, bf16[4,256,384]{2,1,0:T(8,128)(2,1)S(1)}, f32[4,8]{1,0:T(4,128)S(1)}) custom-call(f32[2,512,384]{2,1,0:T(8,128)} %cot_hbm.1, bf16[4,256,384]{2,1,0:T(8,128)(2,1)} %amp_hbm.1, bf16[4,256,384]{2,1,0:T(8,128)(2,1)} %phase_hbm.1, s32[4,48,256]{2,1,0:T(8,128)} %bitcast.3, f32[4,8]{1,0:T(4,128)} %bitcast.4, ...), custom_call_target="tpu_custom_call" | custom-call | tf_op jit(solution)/shard_map/pallas_call | solution.py:450
  92.0 1.2 %shard_map.86 = (bf16[4,256,384]{2,1,0:T(8,128)(2,1)}, bf16[4,256,384]{2,1,0:T(8,128)(2,1)}, f32[4,8]{1,0:T(4,128)}) custom-call(bf16[4,256,384]{2,1,0:T(8,128)(2,1)S(1)} %get-tuple-element.9.amp_in, bf16[4,256,384]{2,1,0:T(8,128)(2,1)S(1)} %get-tuple-element.10.phase_in, f32[4,8]{1,0:T(4,128)S(1)} %get-tuple-element.11.layers_in), custom_call_target="tpu_custom_call" | custom-call | tf_op jit(solution)/shard_map/pallas_call | solution.py:486
